TPU v7x, 32 devices: a whole 2x2x4 slice. The times are simulated.
32 devices in a mesh: lon: 8 (over z, x), lat: 4 (over y, core).
Axes of the slice: x: 2, y: 2, z: 4, core: 2. Of those that a mesh axis runs over, the one named last changes fastest.
Arguments:
- adj_elev: float32 [1280, 5120], P('lon', 'lat'), may hold values from -6 to 6
- adj_east: float32 [1280, 5120], P('lon', 'lat'), may hold values from -6 to 6
- adj_north: float32 [1280, 5120], P('lon', 'lat'), may hold values from -6 to 6
- depth: float32 [1280, 5120], P('lon', 'lat'), may hold values from 0.5 to 2
- friction: float32 [1280, 5120], P('lon', 'lat'), may hold values from 0.01 to 0.3
- ocean_mask: int32 [1280, 5120], P('lon', 'lat'), may hold values 0 or 1
- misfit_values: float32 [4, 8192, 256], P(None, ('lon', 'lat')), may hold values from -6 to 6
- dest_lon: int32 [4, 8192, 1], P(None, ('lon', 'lat')), may hold values from 0 to 7; in each aligned block of 256 rows (0 to 255, 256 to 511, ..., all dimensions but the last counted through in order) at most 64 rows name the same one
- block_cell: int32 [4, 8192], P(None, ('lon', 'lat')), may hold values from 0 to 799
Outputs:
- out_elev: float32 [1280, 5120], P('lon', 'lat')
- out_east: float32 [1280, 5120], P('lon', 'lat')
- out_north: float32 [1280, 5120], P('lon', 'lat')
Inputs may be any that keep to these rules, and one draw needn't show every extreme that they name: `dest_lon`: in each step, the 256 rows of one pass owner name each longitude tile at most 64 times, and some owner reaches 64. `block_cell`: several blocks may name the same cell block.
All inputs are finite; a program needn't handle non-finite values. No bound on the sum of `ocean_mask` on one device may be relied on, other than what follows from the above.
Results may differ from a plain program's by a relative error of at most 0.00002.
Values sent between devices are 32-bit elements; how exact they have to be, the bound alone decides.
A program may use at most 128 MiB of HBM per device.

v0:
```python
import functools

import jax
import jax.numpy as jnp
from jax import lax
from jax.experimental import pallas as pl
from jax.experimental.pallas import tpu as pltpu
from jax.sharding import PartitionSpec as P

F32, BF16 = jnp.float32, jnp.bfloat16
MESH = pl.DeviceIdType.MESH
SIDE = 16
NT = (((1,), (1,)), ((), ()))


def split(x):
    high = x.astype(BF16)
    return high, (x - high.astype(F32)).astype(BF16)


def iota(shape, dim):
    return lax.broadcasted_iota(jnp.int32, shape, dim)


def hot(condition):
    return jnp.where(condition, 1.0, 0.0).astype(BF16)


def kernel(
    n_lon, n_lat,
    values, meta, elev_in, east_in, north_in, depth_in, friction_in, mask_in,
    out_e, out_u, out_v,
    send, recv, cell_send, cell_recv, cells, spread, turned, mixed,
    elev, depth, friction, mask, col_n, col_s,
    to_w, to_e, to_s, to_n, from_e, from_w, from_n, from_s,
    load_sem, send_sem, recv_sem, cell_sems, halo_send, halo_recv,
):
    steps, owned, width = values.shape
    rows, cols = out_e.shape
    slots = 2 * owned // n_lon
    total = n_lon * slots
    per_lane = 128 // slots
    n_bi, n_bj = rows // SIDE, cols // SIDE
    wide = to_s.shape[-1]
    lon, lat = lax.axis_index("lon"), lax.axis_index("lat")

    loads = [
        pltpu.make_async_copy(src, dst, load_sem.at[i])
        for i, (src, dst) in enumerate((
            (elev_in, elev.at[pl.ds(0, rows), :]), (east_in, out_u), (north_in, out_v),
            (depth_in, depth), (friction_in, friction), (mask_in, mask),
        ))
    ]
    for load in loads:
        load.start()

    barrier = pltpu.get_barrier_semaphore()

    def peer(k):
        return lax.rem(lon + k, n_lon)

    @pl.loop(1, n_lon)
    def _(k):
        pl.semaphore_signal(barrier, inc=1, device_id={"lon": peer(k)}, device_id_type=MESH)

    north_of, south_of = lax.rem(lat + 1, n_lat), lax.rem(lat + n_lat - 1, n_lat)
    for there in (north_of, south_of):
        pl.semaphore_signal(barrier, inc=1, device_id={"lat": there}, device_id_type=MESH)

    lower = hot(iota((owned, owned), 0) < iota((owned, owned), 1))
    shift = lax.rem(lon * slots, 128)

    def placed(s):
        dest = meta[s][0:1, :]
        picked = hot(iota((n_lon, owned), 0) == dest)
        before = jnp.dot(picked, lower, preferred_element_type=F32)
        place = jnp.sum(before * picked.astype(F32), axis=0, keepdims=True)
        return dest, place.astype(jnp.int32)

    bundle = jnp.zeros((n_lon * 8, 128), F32)
    for s in range(steps):
        dest, place = placed(s)
        at = iota((8, owned), 0)
        info = meta[s].astype(F32)
        line = jnp.where(at == s, info[1:2, :], jnp.where(at == steps + s, info[2:3, :], 0.0))
        line = jnp.concatenate([line] * n_lon, axis=0)
        line = jnp.where((iota((n_lon * 8, owned), 0) >> 3) == dest, line, 0.0).astype(BF16)
        lane = hot(iota((128, owned), 0) == place + shift)
        bundle = bundle + lax.dot_general(line, lane, NT, preferred_element_type=F32)
    cell_send[...] = bundle.reshape(n_lon, 8, 128)

    pl.semaphore_wait(barrier, n_lon + 1)

    @pl.loop(1, n_lon)
    def _(k):
        pltpu.make_async_remote_copy(
            src_ref=cell_send.at[peer(k)], dst_ref=cell_recv.at[lon],
            send_sem=cell_sems.at[0], recv_sem=cell_sems.at[1],
            device_id={"lon": peer(k)}, device_id_type=MESH,
        ).start()

    @pl.loop(0, steps)
    def _(i):
        s = steps - 1 - i
        dest, place = placed(s)
        pick = hot(iota((total, owned), 0) == dest * slots + place)
        high, low = split(values[s])
        send[s] = jnp.dot(pick, high, preferred_element_type=F32) + jnp.dot(
            pick, low, preferred_element_type=F32
        )

        @pl.loop(1, n_lon)
        def _(k):
            pltpu.make_async_remote_copy(
                src_ref=send.at[s, pl.ds(peer(k) * slots, slots), :],
                dst_ref=recv.at[s, pl.ds(lon * slots, slots), :],
                send_sem=send_sem.at[s], recv_sem=recv_sem.at[s],
                device_id={"lon": peer(k)}, device_id_type=MESH,
            ).start()

        mine = pl.ds(pl.multiple_of(lon * slots, 8), slots)
        recv[s, mine, :] = send[s, mine, :]

    cell_recv[lon] = cell_send[lon]

    for b in range(SIDE):
        spread[b * 128:(b + 1) * 128, :] = hot(iota((128, cols), 1) == iota((128, cols), 0) * SIDE + b)
    at = iota((width, width), 0)
    turn = hot(iota((width, width), 1) == (at % SIDE) * SIDE + at // SIDE)
    eye = iota((rows, wide), 0) == iota((rows, wide), 1)

    def laid(column):
        return jnp.sum(jnp.where(eye, column, 0.0), axis=0, keepdims=True)

    def stood(line):
        return jnp.sum(jnp.where(eye, line, 0.0), axis=1, keepdims=True)

    for load in loads:
        load.wait()

    others = pl.ds(0, n_lon - 1)
    pltpu.make_async_copy(cell_recv.at[others], cell_recv.at[others], cell_sems.at[1]).wait()
    for g in range(total // 128):
        part = cell_recv[g * per_lane:(g + 1) * per_lane]
        cells[:, g * 128:(g + 1) * 128] = jnp.sum(part, axis=0)

    last = jnp.where(lat == n_lat - 1, 1, 0)
    open_lat = jnp.where(lat == 0, 0.0, 1.0)
    most = pl.ds(0, (n_lon - 1) * slots)
    end = cols - 128

    @pl.loop(0, steps)
    def _(i):
        s = steps - 1 - i
        pltpu.make_async_copy(recv.at[s, most, :], recv.at[s, most, :], recv_sem.at[s]).wait()
        bi = cells[pl.ds(s, 1), :].astype(jnp.int32)
        bj = cells[pl.ds(steps + s, 1), :].astype(jnp.int32)
        for h, part in enumerate(split(recv[s])):
            turned[h] = lax.dot_general(turn, part, NT, preferred_element_type=F32).astype(BF16)
        keep = hot((iota((rows, total), 0) // SIDE) == bi)
        column = hot(iota((128, total), 0) == bj)
        for b in range(SIDE):
            both = jnp.concatenate(
                [jnp.concatenate([turned[h, b * SIDE:(b + 1) * SIDE, :]] * n_bi, axis=0) * keep for h in range(2)],
                axis=0,
            )
            got = lax.dot_general(both, column, NT, preferred_element_type=F32)
            high, low = split(got[:rows] + got[rows:])
            mixed[:rows, b * 128:(b + 1) * 128] = high
            mixed[rows:, b * 128:(b + 1) * 128] = low
        for n in range(cols // 256):
            here = slice(n * 256, (n + 1) * 256)
            force = jnp.dot(mixed[...], spread[:, here], preferred_element_type=F32)
            elev[:rows, here] = elev[:rows, here] + mask[:, here].astype(F32) * (force[:rows] + force[rows:])

        to_w[s] = elev[0:1, :]
        to_e[s, :, 0:cols] = elev[rows - 1:rows, :]
        to_e[s, :, cols:2 * cols] = out_u[rows - 1:rows, :]
        to_e[s, :, 2 * cols:] = depth[rows - 1:rows, :] * mask[rows - 1:rows, :].astype(F32)
        first = laid(elev[:rows, 0:128][:, 0:1])
        to_s[s] = first
        to_n[s, :, 0:wide] = laid(elev[:rows, end:][:, 127:128])
        to_n[s, :, wide:2 * wide] = laid(out_v[:, end:][:, 127:128])
        to_n[s, :, 2 * wide:] = laid((depth[:, end:] * mask[:, end:].astype(F32))[:, 127:128])
        copies = [
            pltpu.make_async_remote_copy(
                src_ref=src.at[s], dst_ref=dst.at[s],
                send_sem=halo_send.at[s, q], recv_sem=halo_recv.at[s, q],
                device_id=there, device_id_type=MESH,
            )
            for q, (src, dst, there) in enumerate((
                (to_w, from_e, {"lon": peer(n_lon - 1)}),
                (to_e, from_w, {"lon": peer(1)}),
                (to_s, from_n, {"lat": south_of}),
                (to_n, from_s, {"lat": north_of}),
            ))
        ]
        for copy in copies:
            copy.start()
        for copy in copies:
            copy.wait()
        elev[rows:rows + 1, :] = from_e[s]
        col_n[...] = stood(from_n[s])
        side = from_s[s]
        col_s[...] = stood(
            open_lat * side[:, 2 * wide:]
            * (side[:, wide:2 * wide] + 0.25 * (first - side[:, 0:wide]))
        )
        edge = from_w[s]
        above = edge[:, 2 * cols:] * (
            edge[:, cols:2 * cols] + 0.25 * (elev[0:1, :] - edge[:, 0:cols])
        )
        row_at, lane_at = iota((8, cols), 0), iota((8, cols), 1)

        def chunk(k, above):
            here = pl.ds(pl.multiple_of(k * 8, 8), 8)
            e = elev[here, :]
            e_next = elev[pl.ds(pl.multiple_of(k * 8 + 8, 8), 8), :]
            wet = mask[here, :].astype(F32)
            wet_v = jnp.where(lane_at < cols - last, wet, 0.0)
            e_east = jnp.where(row_at == 7, e_next[0:1, :], pltpu.roll(e, 7, 0))
            e_north = jnp.where(lane_at == cols - 1, col_n[here, :], pltpu.roll(e, cols - 1, 1))
            flow_u = wet * (out_u[here, :] + 0.25 * (e_east - e))
            flow_v = wet_v * (out_v[here, :] + 0.25 * (e_north - e))
            deep = depth[here, :]
            term_u, term_v = deep * flow_u, deep * flow_v
            west = jnp.where(row_at == 0, above, pltpu.roll(term_u, 1, 0))
            south = jnp.where(lane_at == 0, col_s[here, :], pltpu.roll(term_v, 1, 1))
            e = e + 0.25 * (term_u - west) + 0.25 * (term_v - south)
            elev[here, :] = e
            out_e[here, :] = e
            slow = 1.0 - friction[here, :]
            out_u[here, :] = slow * flow_u
            out_v[here, :] = slow * flow_v
            return term_u[7:8, :]

        lax.fori_loop(0, rows // 8, chunk, above)

    pltpu.make_async_copy(cell_send.at[others], cell_send.at[others], cell_sems.at[0]).wait()

    @pl.loop(0, steps)
    def _(s):
        pltpu.make_async_copy(send.at[s, most, :], send.at[s, most, :], send_sem.at[s]).wait()


def per_device(
    n_lon, n_lat,
    adj_elev, adj_east, adj_north, depth, friction, ocean_mask, misfit_values, dest_lon, block_cell,
):
    rows, cols = adj_elev.shape
    steps, owned, width = misfit_values.shape
    slots = 2 * owned // n_lon
    total = n_lon * slots
    per_lat = cols // SIDE
    meta = jnp.stack([dest_lon[:, :, 0], block_cell // per_lat, block_cell % per_lat], axis=1)
    meta = jnp.pad(meta, ((0, 0), (0, 5), (0, 0)))
    wide = -(-rows // 128) * 128
    vmem = pl.BlockSpec(memory_space=pltpu.VMEM)
    hbm = pl.BlockSpec(memory_space=pl.ANY)
    tile = jax.ShapeDtypeStruct((rows, cols), F32)
    return pl.pallas_call(
        functools.partial(kernel, n_lon, n_lat),
        out_shape=(tile, tile, tile),
        in_specs=[vmem] * 2 + [hbm] * 6,
        out_specs=(vmem, vmem, vmem),
        scratch_shapes=[
            pltpu.VMEM((steps, total, width), F32),
            pltpu.VMEM((steps, total, width), F32),
            pltpu.VMEM((n_lon, 8, 128), F32),
            pltpu.VMEM((n_lon, 8, 128), F32),
            pltpu.VMEM((8, total), F32),
            pltpu.VMEM((SIDE * 128, cols), BF16),
            pltpu.VMEM((2, width, total), BF16),
            pltpu.VMEM((2 * rows, SIDE * 128), BF16),
            pltpu.VMEM((rows + 8, cols), F32),
            pltpu.VMEM((rows, cols), F32),
            pltpu.VMEM((rows, cols), F32),
            pltpu.VMEM((rows, cols), jnp.int32),
            pltpu.VMEM((rows, 1), F32),
            pltpu.VMEM((rows, 1), F32),
            pltpu.VMEM((steps, 1, cols), F32),
            pltpu.VMEM((steps, 1, 3 * cols), F32),
            pltpu.VMEM((steps, 1, wide), F32),
            pltpu.VMEM((steps, 1, 3 * wide), F32),
            pltpu.VMEM((steps, 1, cols), F32),
            pltpu.VMEM((steps, 1, 3 * cols), F32),
            pltpu.VMEM((steps, 1, wide), F32),
            pltpu.VMEM((steps, 1, 3 * wide), F32),
            pltpu.SemaphoreType.DMA((6,)),
            pltpu.SemaphoreType.DMA((steps,)),
            pltpu.SemaphoreType.DMA((steps,)),
            pltpu.SemaphoreType.DMA((2,)),
            pltpu.SemaphoreType.DMA((steps, 4)),
            pltpu.SemaphoreType.DMA((steps, 4)),
        ],
        compiler_params=pltpu.CompilerParams(
            collective_id=0, has_side_effects=True, vmem_limit_bytes=48 * 2**20
        ),
    )(misfit_values, meta, adj_elev, adj_east, adj_north, depth, friction, ocean_mask)


def solution(mesh):
    tile, owned = P("lon", "lat"), P(None, ("lon", "lat"))
    return jax.shard_map(
        functools.partial(per_device, mesh.shape["lon"], mesh.shape["lat"]),
        mesh=mesh,
        in_specs=(tile,) * 6 + (P(None, ("lon", "lat"), None), P(None, ("lon", "lat"), None), owned),
        out_specs=(tile, tile, tile),
        check_vma=False,
    )
```

profile of v0, /device:TPU:0, one launch (start us, length us, event | category | flops | bytes accessed | tf_op | source)
XLA Modules:
  0.0 97.7 jit_solution(14248976383228713683)
XLA Ops:
  0.6 0.7 fusion
  1.3 0.0 copy-start.4
  1.4 0.7 copy-done.4
  2.1 0.0 copy-start
  2.1 1.1 %copy-done = f32[160,1280]{1,0:T(8,128)S(1)} copy-done((f32[160,1280]{1,0:T(8,128)S(1)}, f32[160,1280]{1,0:T(8,128)}, u32[]{:S(2)}) %copy-start) | copy-done | bytes 819224
  3.2 0.0 copy-start.1
  3.2 1.1 %copy-done.1 = f32[160,1280]{1,0:T(8,128)S(1)} copy-done((f32[160,1280]{1,0:T(8,128)S(1)}, f32[160,1280]{1,0:T(8,128)}, u32[]{:S(2)}) %copy-start.1) | copy-done | bytes 819224
  4.4 0.0 copy-start.2
  4.4 1.1 %copy-done.2 = f32[160,1280]{1,0:T(8,128)S(1)} copy-done((f32[160,1280]{1,0:T(8,128)S(1)}, f32[160,1280]{1,0:T(8,128)}, u32[]{:S(2)}) %copy-start.2) | copy-done | bytes 819224
  5.5 0.0 copy-start.3
  5.5 1.1 %copy-done.3 = f32[160,1280]{1,0:T(8,128)S(1)} copy-done((f32[160,1280]{1,0:T(8,128)S(1)}, f32[160,1280]{1,0:T(8,128)}, u32[]{:S(2)}) %copy-start.3) | copy-done | bytes 819224
  6.7 88.4 %shard_map.112 = (f32[160,1280]{1,0:T(8,128)S(1)}, f32[160,1280]{1,0:T(8,128)S(1)}, f32[160,1280]{1,0:T(8,128)S(1)}) custom-call(f32[4,256,256]{2,1,0:T(8,128)} %values.1, s32[4,8,256]{2,1,0:T(8,128)S(1)} %pad.4.meta, f32[160,1280]{1,0:T(8,128)S(1)} %copy-done, f32[160,1280]{1,0:T(8,128)S(1)} %copy-done.1, f32[160,1280]{1,0:T(8,128)S(1)} %copy-done.2, ...), custom_call_target="tpu_custom_call" | custom-call | tf_op jit(solution)/shard_map/pallas_call | solution.py:261
  95.0 0.9 copy.16
  95.9 0.9 copy.17
  96.8 0.9 copy.18
  (4 shorter events, 0.0 us)
Async XLA Ops:
  1.3 0.7 copy-start.4
  2.1 1.1 %copy-start = (f32[160,1280]{1,0:T(8,128)S(1)}, f32[160,1280]{1,0:T(8,128)}, u32[]{:S(2)}) copy-start(f32[160,1280]{1,0:T(8,128)} %elev_in.1) | copy-start | bytes 2457604
  3.2 1.1 %copy-start.1 = (f32[160,1280]{1,0:T(8,128)S(1)}, f32[160,1280]{1,0:T(8,128)}, u32[]{:S(2)}) copy-start(f32[160,1280]{1,0:T(8,128)} %east_in.1) | copy-start | bytes 2457604
  4.4 1.1 %copy-start.2 = (f32[160,1280]{1,0:T(8,128)S(1)}, f32[160,1280]{1,0:T(8,128)}, u32[]{:S(2)}) copy-start(f32[160,1280]{1,0:T(8,128)} %north_in.1) | copy-start | bytes 2457604
  5.5 1.1 %copy-start.3 = (f32[160,1280]{1,0:T(8,128)S(1)}, f32[160,1280]{1,0:T(8,128)}, u32[]{:S(2)}) copy-start(f32[160,1280]{1,0:T(8,128)} %depth_in.1) | copy-start | bytes 2457604
where the time goes:
time: 98.1 us; the launch traced here: 97.7 us
  Pallas kernels  88.4 us (90%)
  local copies, waits for them, and re-layouts  7.93 us (8%)
    pallas_call x1, Pallas kernels, per_device(): pl.pallas_call(functools.partial(kernel, n_lon, n_lat), out_shape=(tile,...  88.4 us
    unnamed x13, local copies, waits for them, and re-layouts  7.92 us

commit v1 on v0

--- a/solution.py
+++ b/solution.py
@@ -30,7 +30,7 @@
     n_lon, n_lat,
     values, meta, elev_in, east_in, north_in, depth_in, friction_in, mask_in,
     out_e, out_u, out_v,
-    send, recv, cell_send, cell_recv, cells, spread, turned, mixed,
+    send, recv, cell_send, cell_recv, cells, spread, turned, mixed, force,
     elev, depth, friction, mask, col_n, col_s,
     to_w, to_e, to_s, to_n, from_e, from_w, from_n, from_s,
     load_sem, send_sem, recv_sem, cell_sems, halo_send, halo_recv,
@@ -149,9 +149,7 @@
     most = pl.ds(0, (n_lon - 1) * slots)
     end = cols - 128
 
-    @pl.loop(0, steps)
-    def _(i):
-        s = steps - 1 - i
+    def scatter(s):
         pltpu.make_async_copy(recv.at[s, most, :], recv.at[s, most, :], recv_sem.at[s]).wait()
         bi = cells[pl.ds(s, 1), :].astype(jnp.int32)
         bj = cells[pl.ds(steps + s, 1), :].astype(jnp.int32)
@@ -170,9 +168,15 @@
             mixed[rows:, b * 128:(b + 1) * 128] = low
         for n in range(cols // 256):
             here = slice(n * 256, (n + 1) * 256)
-            force = jnp.dot(mixed[...], spread[:, here], preferred_element_type=F32)
-            elev[:rows, here] = elev[:rows, here] + mask[:, here].astype(F32) * (force[:rows] + force[rows:])
-
+            got = jnp.dot(mixed[...], spread[:, here], preferred_element_type=F32)
+            force[s, :, here] = mask[:, here].astype(F32) * (got[:rows] + got[rows:])
+
+    scatter(steps - 1)
+
+    @pl.loop(0, steps)
+    def _(i):
+        s = steps - 1 - i
+        elev[:rows, :] = elev[:rows, :] + force[s]
         to_w[s] = elev[0:1, :]
         to_e[s, :, 0:cols] = elev[rows - 1:rows, :]
         to_e[s, :, cols:2 * cols] = out_u[rows - 1:rows, :]
@@ -197,6 +201,11 @@
         ]
         for copy in copies:
             copy.start()
+
+        @pl.when(i < steps - 1)
+        def _():
+            scatter(s - 1)
+
         for copy in copies:
             copy.wait()
         elev[rows:rows + 1, :] = from_e[s]
@@ -272,6 +281,7 @@
             pltpu.VMEM((SIDE * 128, cols), BF16),
             pltpu.VMEM((2, width, total), BF16),
             pltpu.VMEM((2 * rows, SIDE * 128), BF16),
+            pltpu.VMEM((steps, rows, cols), F32),
             pltpu.VMEM((rows + 8, cols), F32),
             pltpu.VMEM((rows, cols), F32),
             pltpu.VMEM((rows, cols), F32),
@@ -294,7 +304,7 @@
             pltpu.SemaphoreType.DMA((steps, 4)),
         ],
         compiler_params=pltpu.CompilerParams(
-            collective_id=0, has_side_effects=True, vmem_limit_bytes=48 * 2**20
+            collective_id=0, has_side_effects=True, vmem_limit_bytes=60 * 2**20
         ),
     )(misfit_values, meta, adj_elev, adj_east, adj_north, depth, friction, ocean_mask)
 

time: 98.1 us -> 86 us (0.88)
  Pallas kernels: 88.4 us -> 78.5 us
  local copies, waits for them, and re-layouts: 7.93 us -> 5.8 us
    pallas_call x1, Pallas kernels: 88.4 us -> 78.5 us  [per_device(): pl.pallas_call(functools.partial(kernel, n_lon, n_lat), out_shape=(tile,...]
    unnamed x13 -> x9, local copies, waits for them, and re-layouts: 7.92 us -> 5.17 us
where the time goes in v1:
time: 86 us; the launch traced here: 85.7 us
  Pallas kernels  78.5 us (91%)
  local copies, waits for them, and re-layouts  5.8 us (7%)
    pallas_call x1, Pallas kernels, per_device(): pl.pallas_call(functools.partial(kernel, n_lon, n_lat), out_shape=(tile,...  78.5 us
    unnamed x9, local copies, waits for them, and re-layouts  5.17 us

profile of v1, /device:TPU:0, one launch (start us, length us, event | category | flops | bytes accessed | tf_op | source)
XLA Modules:
  0.0 85.7 jit_solution(2798911594264240429)
XLA Ops:
  0.6 0.7 fusion
  1.3 0.0 copy-start.2
  1.4 0.7 copy-done.2
  2.1 0.6 pad.4.meta
  2.7 78.5 %shard_map.112 = (f32[160,1280]{1,0:T(8,128)}, f32[160,1280]{1,0:T(8,128)}, f32[160,1280]{1,0:T(8,128)}) custom-call(f32[4,256,256]{2,1,0:T(8,128)} %values.1, s32[4,8,256]{2,1,0:T(8,128)} %pad.4.meta, f32[160,1280]{1,0:T(8,128)} %elev_in.1, f32[160,1280]{1,0:T(8,128)} %east_in.1, f32[160,1280]{1,0:T(8,128)} %north_in.1, f32[160,1280]{1,0:T(8,128)} %depth_in.1, ...), custom_call_target="tpu_custom_call" | custom-call | tf_op jit(solution)/shard_map/pallas_call | solution.py:270
  81.2 0.0 copy-start.1
  81.2 2.2 %copy.16 = f32[160,1280]{1,0:T(8,128)} copy(f32[160,1280]{1,0:T(8,128)} %get-tuple-element.8) | data formatting | bytes 1638400
  83.3 0.0 copy-done.1
  83.3 0.0 copy-start
  83.3 0.9 %copy.17 = f32[160,1280]{1,0:T(8,128)} copy(f32[160,1280]{1,0:T(8,128)S(1)} %copy-done.1) | data formatting | bytes 1638400
  84.2 0.5 copy-done
  84.8 0.9 %copy.18 = f32[160,1280]{1,0:T(8,128)} copy(f32[160,1280]{1,0:T(8,128)S(1)} %copy-done) | data formatting | bytes 1638400
  (3 shorter events, 0.0 us)
Async XLA Ops:
  1.3 0.7 copy-start.2
  81.2 2.2 %copy-start.1 = (f32[160,1280]{1,0:T(8,128)S(1)}, f32[160,1280]{1,0:T(8,128)}, u32[]{:S(2)}) copy-start(f32[160,1280]{1,0:T(8,128)} %get-tuple-element.9) | copy-start | bytes 2457604
  83.3 1.4 %copy-start = (f32[160,1280]{1,0:T(8,128)S(1)}, f32[160,1280]{1,0:T(8,128)}, u32[]{:S(2)}) copy-start(f32[160,1280]{1,0:T(8,128)} %get-tuple-element.10) | copy-start | bytes 2457604

commit v2 on v1

--- a/solution.py
+++ b/solution.py
@@ -99,6 +99,16 @@
             device_id={"lon": peer(k)}, device_id_type=MESH,
         ).start()
 
+    def post(s):
+        @pl.loop(1, n_lon)
+        def _(k):
+            pltpu.make_async_remote_copy(
+                src_ref=send.at[s, pl.ds(peer(k) * slots, slots), :],
+                dst_ref=recv.at[s, pl.ds(lon * slots, slots), :],
+                send_sem=send_sem.at[s], recv_sem=recv_sem.at[s],
+                device_id={"lon": peer(k)}, device_id_type=MESH,
+            ).start()
+
     @pl.loop(0, steps)
     def _(i):
         s = steps - 1 - i
@@ -109,14 +119,9 @@
             pick, low, preferred_element_type=F32
         )
 
-        @pl.loop(1, n_lon)
-        def _(k):
-            pltpu.make_async_remote_copy(
-                src_ref=send.at[s, pl.ds(peer(k) * slots, slots), :],
-                dst_ref=recv.at[s, pl.ds(lon * slots, slots), :],
-                send_sem=send_sem.at[s], recv_sem=recv_sem.at[s],
-                device_id={"lon": peer(k)}, device_id_type=MESH,
-            ).start()
+        @pl.when(i < 2)
+        def _():
+            post(s)
 
         mine = pl.ds(pl.multiple_of(lon * slots, 8), slots)
         recv[s, mine, :] = send[s, mine, :]
@@ -201,6 +206,10 @@
         ]
         for copy in copies:
             copy.start()
+
+        @pl.when(i < steps - 2)
+        def _():
+            post(s - 2)
 
         @pl.when(i < steps - 1)
         def _():

time: 86 us -> 81.9 us (0.952)
  Pallas kernels: 78.5 us -> 74.5 us
    pallas_call x1, Pallas kernels: 78.5 us -> 74.5 us  [per_device(): pl.pallas_call(functools.partial(kernel, n_lon, n_lat), out_shape=(tile,...]
where the time goes in v2:
time: 81.9 us; the launch traced here: 81.7 us
  Pallas kernels  74.5 us (91%)
  local copies, waits for them, and re-layouts  5.8 us (7%)
    pallas_call x1, Pallas kernels, per_device(): pl.pallas_call(functools.partial(kernel, n_lon, n_lat), out_shape=(tile,...  74.5 us
    unnamed x9, local copies, waits for them, and re-layouts  5.17 us

profile of v2, /device:TPU:0, one launch (start us, length us, event | category | flops | bytes accessed | tf_op | source)
XLA Modules:
  0.0 81.7 jit_solution(2856850232062378322)
XLA Ops:
  0.6 0.7 fusion
  1.3 0.0 copy-start.2
  1.4 0.7 copy-done.2
  2.1 0.6 pad.4.meta
  2.7 74.5 %shard_map.112 = (f32[160,1280]{1,0:T(8,128)}, f32[160,1280]{1,0:T(8,128)}, f32[160,1280]{1,0:T(8,128)}) custom-call(f32[4,256,256]{2,1,0:T(8,128)} %values.1, s32[4,8,256]{2,1,0:T(8,128)} %pad.4.meta, f32[160,1280]{1,0:T(8,128)} %elev_in.1, f32[160,1280]{1,0:T(8,128)} %east_in.1, f32[160,1280]{1,0:T(8,128)} %north_in.1, f32[160,1280]{1,0:T(8,128)} %depth_in.1, ...), custom_call_target="tpu_custom_call" | custom-call | tf_op jit(solution)/shard_map/pallas_call | solution.py:279
  77.1 0.0 copy-start.1
  77.2 2.2 %copy.16 = f32[160,1280]{1,0:T(8,128)} copy(f32[160,1280]{1,0:T(8,128)} %get-tuple-element.8) | data formatting | bytes 1638400
  79.3 0.0 copy-done.1
  79.3 0.0 copy-start
  79.3 0.9 %copy.17 = f32[160,1280]{1,0:T(8,128)} copy(f32[160,1280]{1,0:T(8,128)S(1)} %copy-done.1) | data formatting | bytes 1638400
  80.2 0.5 copy-done
  80.8 0.9 %copy.18 = f32[160,1280]{1,0:T(8,128)} copy(f32[160,1280]{1,0:T(8,128)S(1)} %copy-done) | data formatting | bytes 1638400
  (3 shorter events, 0.0 us)
Async XLA Ops:
  1.3 0.7 copy-start.2
  77.1 2.2 %copy-start.1 = (f32[160,1280]{1,0:T(8,128)S(1)}, f32[160,1280]{1,0:T(8,128)}, u32[]{:S(2)}) copy-start(f32[160,1280]{1,0:T(8,128)} %get-tuple-element.9) | copy-start | bytes 2457604
  79.3 1.4 %copy-start = (f32[160,1280]{1,0:T(8,128)S(1)}, f32[160,1280]{1,0:T(8,128)}, u32[]{:S(2)}) copy-start(f32[160,1280]{1,0:T(8,128)} %get-tuple-element.10) | copy-start | bytes 2457604

commit v3 on v2

--- a/solution.py
+++ b/solution.py
@@ -252,7 +252,7 @@
             out_v[here, :] = slow * flow_v
             return term_u[7:8, :]
 
-        lax.fori_loop(0, rows // 8, chunk, above)
+        lax.fori_loop(0, rows // 8, chunk, above, unroll=4)
 
     pltpu.make_async_copy(cell_send.at[others], cell_send.at[others], cell_sems.at[0]).wait()
 

time: 81.9 us -> 81.9 us (level)
  no operation moved by 1% of the time
where the time goes in v3:
time: 81.9 us; the launch traced here: 81.6 us
  Pallas kernels  74.4 us (91%)
  local copies, waits for them, and re-layouts  5.8 us (7%)
    pallas_call x1, Pallas kernels, per_device(): pl.pallas_call(functools.partial(kernel, n_lon, n_lat), out_shape=(tile,...  74.4 us
    unnamed x9, local copies, waits for them, and re-layouts  5.17 us

profile of v3, /device:TPU:0, one launch (start us, length us, event | category | flops | bytes accessed | tf_op | source)
XLA Modules:
  0.0 81.6 jit_solution(3238704389452465988)
XLA Ops:
  0.6 0.7 fusion
  1.3 0.0 copy-start.2
  1.4 0.7 copy-done.2
  2.1 0.6 pad.4.meta
  2.7 74.4 %shard_map.112 = (f32[160,1280]{1,0:T(8,128)}, f32[160,1280]{1,0:T(8,128)}, f32[160,1280]{1,0:T(8,128)}) custom-call(f32[4,256,256]{2,1,0:T(8,128)} %values.1, s32[4,8,256]{2,1,0:T(8,128)} %pad.4.meta, f32[160,1280]{1,0:T(8,128)} %elev_in.1, f32[160,1280]{1,0:T(8,128)} %east_in.1, f32[160,1280]{1,0:T(8,128)} %north_in.1, f32[160,1280]{1,0:T(8,128)} %depth_in.1, ...), custom_call_target="tpu_custom_call" | custom-call | tf_op jit(solution)/shard_map/pallas_call | solution.py:279
  77.1 0.0 copy-start.1
  77.1 2.2 %copy.16 = f32[160,1280]{1,0:T(8,128)} copy(f32[160,1280]{1,0:T(8,128)} %get-tuple-element.8) | data formatting | bytes 1638400
  79.3 0.0 copy-done.1
  79.3 0.0 copy-start
  79.3 0.9 %copy.17 = f32[160,1280]{1,0:T(8,128)} copy(f32[160,1280]{1,0:T(8,128)S(1)} %copy-done.1) | data formatting | bytes 1638400
  80.2 0.5 copy-done
  80.7 0.9 %copy.18 = f32[160,1280]{1,0:T(8,128)} copy(f32[160,1280]{1,0:T(8,128)S(1)} %copy-done) | data formatting | bytes 1638400
  (3 shorter events, 0.0 us)
Async XLA Ops:
  1.3 0.7 copy-start.2
  77.1 2.2 %copy-start.1 = (f32[160,1280]{1,0:T(8,128)S(1)}, f32[160,1280]{1,0:T(8,128)}, u32[]{:S(2)}) copy-start(f32[160,1280]{1,0:T(8,128)} %get-tuple-element.9) | copy-start | bytes 2457604
  79.3 1.4 %copy-start = (f32[160,1280]{1,0:T(8,128)S(1)}, f32[160,1280]{1,0:T(8,128)}, u32[]{:S(2)}) copy-start(f32[160,1280]{1,0:T(8,128)} %get-tuple-element.10) | copy-start | bytes 2457604
